TPU v7x, 256 devices: a whole 4x4x8 slice. The times are simulated.
256 devices in a mesh: group: 8 (over x, core), sub: 32 (over y, z).
Axes of the slice: x: 4, y: 4, z: 8, core: 2. Of those that a mesh axis runs over, the one named last changes fastest.
Arguments:
- resid_iface: float32 [256, 16, 4352], P(('group', 'sub')), may hold values from -6 to 6
- resid_inner: float32 [256, 16, 3072], P(('group', 'sub')), may hold values from -6 to 6
- weights: float32 [256, 4352], P(('group', 'sub')), may hold values from 0.25 to 0.75
- nbr: int32 [256, 32], P(('group', 'sub')), may hold values from 0 to 1, as said below
- own2: int32 [256, 128], P(('group', 'sub')), may hold values from 0 to 2047
- cidx: int32 [256, 8], P(('group', 'sub')), may hold values from 0 to 16
- neumann: bfloat16 [256, 17, 256, 256], P(('group', 'sub'))
- dirichlet: bfloat16 [256, 8, 384, 384], P(('group', 'sub'))
- coupling: bfloat16 [256, 8, 256, 384], P(('group', 'sub')), may hold values from -0.375 to 0.375
- coarse_basis: bfloat16 [256, 4352, 128], P(('group', 'sub')), may hold values from -0.5 to 0.5
- group_basis: float32 [16384, 512], P(('group', 'sub')), may hold values from -0.25 to 0.25
- group_inverse: float32 [16384, 2048], P('group', 'sub'), as said below
- top_inverse: float32 [512, 512], replicated, as said below
Outputs:
- interface_out: float32 [256, 16, 4352], P(('group', 'sub'))
- interior_out: float32 [256, 16, 3072], P(('group', 'sub'))
Inputs may be any that keep to these rules, and one draw needn't show every extreme that they name: Symmetric within each group (nbr[(g, q), j] = nbr[(g, j), q]) with nbr[(g, q), q] = 0. `group_inverse`: each matrix of a group is symmetric. `top_inverse`: symmetric.
All inputs are finite; a program needn't handle non-finite values.
Results may differ from a plain program's by a relative error of at most 0.013.
Values may be sent and summed in bfloat16 or wider, within the bound.
A program may use at most 64 MiB of HBM per device.

v0:
```python
import jax
import jax.numpy as jnp
from jax import lax
from jax.sharding import PartitionSpec as P


def padded_2(cells, sides, width):
    for axis, dim in sides:
        count = lax.axis_size(axis)
        ends = count - 1
        head = lax.slice_in_dim(cells, 0, width, axis=dim)
        tail = lax.slice_in_dim(cells, cells.shape[dim] - width, cells.shape[dim], axis=dim)
        cells = jnp.concatenate(
            [
                lax.ppermute(tail, axis, [(i, (i + 1) % count) for i in range(ends)]),
                cells,
                lax.ppermute(head, axis, [((i + 1) % count, i) for i in range(ends)]),
            ],
            axis=dim,
        )
    return cells


def shards(
    resid_iface,
    resid_inner,
    weights,
    nbr,
    own2,
    cidx,
    neumann,
    dirichlet,
    coupling,
    coarse_basis,
    group_basis,
    group_inverse,
    top_inverse,
):
    highest = lax.Precision.HIGHEST
    nsub = lax.axis_size("sub")
    mine = lax.axis_index("sub")
    rows = resid_iface.shape[1]
    width = resid_iface.shape[2]
    slot_width = width // (nsub + 2)
    block_count = neumann.shape[1]
    block_width = neumann.shape[2]
    inner_count = dirichlet.shape[1]
    inner_width = dirichlet.shape[2]
    group_width = group_inverse.shape[0]
    share = group_inverse.shape[1]
    slot_mask = jnp.concatenate([nbr[0].astype(jnp.float32), jnp.ones((2,), jnp.float32)])
    scale = jnp.repeat(slot_mask, slot_width) * weights[0]
    weighted = (scale[None, :] * resid_iface[0]).astype(jnp.bfloat16)
    local0 = jnp.dot(weighted, coarse_basis[0], preferred_element_type=jnp.float32)
    onehot = (own2[0][:, None] == jnp.arange(group_width, dtype=jnp.int32)[None, :]).astype(
        jnp.float32
    )
    contrib = jnp.dot(local0, onehot, precision=highest)
    level2 = lax.psum(contrib.astype(jnp.bfloat16), "sub").astype(jnp.float32)
    level2_mine = lax.dynamic_slice_in_dim(level2, mine * share, share, 1)
    neumann_part = jnp.einsum(
        "rkb,kbc->rkc",
        weighted.reshape(rows, block_count, block_width),
        neumann[0],
        preferred_element_type=jnp.float32,
    ).reshape(rows, width)
    top_term = jnp.dot(level2_mine, group_basis, precision=highest)
    level3 = lax.psum(top_term, ("group", "sub"))
    coarse3 = jnp.dot(level3, top_inverse, precision=highest)
    lifted = lax.dot_general(coarse3, group_basis, (((1,), (1,)), ((), ())), precision=highest)
    coarse2_mine = jnp.dot(level2, group_inverse, precision=highest) + lifted
    coarse2 = lax.all_gather(coarse2_mine.astype(jnp.bfloat16), "sub", axis=1, tiled=True)
    values = jnp.take(coarse2, own2[0], axis=1)
    spread = lax.dot_general(
        values, coarse_basis[0], (((1,), (1,)), ((), ())), preferred_element_type=jnp.float32
    )
    scaled = scale[None, :] * (neumann_part + spread)
    slots = scaled.reshape(rows, nsub + 2, slot_width)
    received = lax.all_to_all(
        slots[:, :nsub, :].astype(jnp.bfloat16), "sub", split_axis=1, concat_axis=1, tiled=True
    ).astype(jnp.float32)
    padded = padded_2(slots[:, nsub:, :], (("group", 1),), 1)
    lower_face = slots[:, nsub, :] + padded[:, 0, :]
    upper_face = slots[:, nsub + 1, :] + padded[:, 3, :]
    total = jnp.concatenate(
        [slots[:, :nsub, :] + received, lower_face[:, None, :], upper_face[:, None, :]], axis=1
    )
    interface_out = total.reshape(rows, width)
    iface_blocks = interface_out.reshape(rows, block_count, block_width).astype(jnp.bfloat16)
    picked = jnp.take(iface_blocks, cidx[0], axis=1)
    pushed = jnp.einsum("rkb,kbc->rkc", picked, coupling[0], preferred_element_type=jnp.float32)
    inner_rhs = (resid_inner[0].reshape(rows, inner_count, inner_width) - pushed).astype(
        jnp.bfloat16
    )
    interior_out = jnp.einsum(
        "rkb,kbc->rkc", inner_rhs, dirichlet[0], preferred_element_type=jnp.float32
    ).reshape(rows, inner_count * inner_width)
    return (interface_out[None], interior_out[None])


def solution(mesh):
    placed = (
        P(("group", "sub"), None, None),
        P(("group", "sub"), None, None),
        P(("group", "sub"), None),
        P(("group", "sub"), None),
        P(("group", "sub"), None),
        P(("group", "sub"), None),
        P(("group", "sub"), None, None, None),
        P(("group", "sub"), None, None, None),
        P(("group", "sub"), None, None, None),
        P(("group", "sub"), None, None),
        P(("group", "sub"), None),
        P("group", "sub"),
        P(),
    )
    return jax.shard_map(
        shards,
        mesh=mesh,
        in_specs=placed,
        out_specs=(P(("group", "sub"), None, None), P(("group", "sub"), None, None)),
        check_vma=False,
    )
```

profile of v0, /device:TPU:1, one launch (start us, length us, event | category | flops | bytes accessed | tf_op | source)
XLA Modules:
  0.0 318.7 jit_solution(4623421728509135453)
XLA Ops:
  7.2 0.0 copy-start
  7.2 0.0 copy-start.2
  7.2 0.0 copy-start.4
  7.2 0.0 copy-start.5
  7.2 0.0 all-reduce.3.cloned.1.call-start
  7.3 0.8 convert_bitcast_fusion
  8.1 0.1 broadcast_bitcast_fusion
  8.1 0.8 fusion.45
  8.9 1.6 fusion.25
  10.5 1.8 convolution_convert_fusion
  12.3 0.0 all-reduce.3.cloned.1.call-update
  12.4 0.0 copy-done.4
  12.4 0.0 copy-done.2
  12.5 0.0 copy-done.5
  12.6 2.0 fusion.7
  14.6 0.7 copy.43
  15.3 0.0 copy-start.1
  15.3 136.0 %all-reduce.3.cloned.1.call-done = bf16[16,2048]{1,0:T(8,128)(2,1)} async-done(((bf16[16,2048]{1,0:T(8,128)(2,1)}), bf16[16,2048]{1,0:T(8,128)(2,1)}) %all-reduce.3.cloned.1.call-update) | async-done | bytes 65552 | tf_op jit(solution)/shard_map/psum | solution.py:59
  151.3 1.7 fusion.47
  153.0 78.0 %psum.15 = f32[16,512]{1,0:T(8,128)S(1)} all-reduce(f32[16,512]{1,0:T(8,128)} %fusion.47), channel_id=1, replica_groups=mesh['group'=8,'sub'=32] {'group','sub'}, use_global_device_ids=true, to_apply=%region_1.0 | all-reduce | flops 8192 | bytes 65536 | tf_op jit(solution)/shard_map/psum | solution.py:68
  231.1 0.0 copy-start.3
  231.1 1.9 fusion.58
  233.0 1.4 fusion.57
  234.4 0.0 copy-done.3
  234.4 0.2 fusion.28
  234.6 35.0 %all-gather = bf16[32,64,16]{1,2,0:T(8,128)(2,1)} all-gather(bf16[1,64,16]{1,2,0:T(8,128)(2,1)S(1)} %fusion.28), channel_id=1, replica_groups=mesh['group'=8,'sub'=32] {'sub'}, dimensions={0}, use_global_device_ids=true | all-gather | bytes 67584 | tf_op jit(solution)/shard_map/all_gather | solution.py:72
  269.6 1.9 copy.41
  271.5 1.8 gather_fusion
  273.3 0.0 copy-done.1
  273.3 2.2 fusion
  275.5 1.0 reshape.101
  276.5 12.7 %collective-permute-start = (f32[16,1,128]{2,1,0:T(1,128)S(1)}, f32[16,1,128]{2,1,0:T(1,128)S(1)}, u32[]{:S(2)}, u32[]{:S(2)}) collective-permute-start(f32[16,1,128]{2,1,0:T(1,128)S(1)} %get-tuple-element.4), channel_id=1, source_target_pairs={{0,32},{32,64},{64,96},{96,128},{128,160},{160,192},{192,224},{1,3... | collective-permute-start | bytes 24584 | tf_op jit(solution)/shard_map/ppermute | solution.py:15
  289.2 1.9 collective-permute-start.1
  291.2 0.7 copy.36
  291.9 5.6 %all-to-all-start = ((bf16[16,32,128]{2,0,1:T(8,128)(2,1)}), bf16[16,32,128]{2,0,1:T(8,128)(2,1)S(1)}, u32[]{:S(2)}, u32[]{:S(2)}) async-start(bf16[16,32,128]{2,0,1:T(8,128)(2,1)} %copy.36), calls=%async_computation | async-start | bytes 262144 | tf_op jit(solution)/shard_map/all_to_all | solution.py:79
  297.5 1.0 copy.45
  298.5 0.0 collective-permute-done
  298.5 0.0 collective-permute-done.1
  298.6 8.8 %all-to-all-done = bf16[16,32,128]{2,0,1:T(8,128)(2,1)S(1)} async-done(((bf16[16,32,128]{2,0,1:T(8,128)(2,1)}), bf16[16,32,128]{2,0,1:T(8,128)(2,1)S(1)}, u32[]{:S(2)}, u32[]{:S(2)}) %all-to-all-start) | async-done | bytes 131104 | tf_op jit(solution)/shard_map/all_to_all | solution.py:79
  307.5 0.1 convert_element_type.48
  307.6 0.6 gather_fusion.1
  308.2 0.0 copy-done
  308.2 2.1 fusion.10
  310.3 0.1 copy.40
  310.4 0.7 broadcast_in_dim_reshape.7
  311.1 0.8 broadcast_in_dim_reshape.6
  (17 shorter events, 0.3 us)
Async XLA Ops:
  7.2 301.0 %copy-start = (bf16[1,8,384,384]{3,2,1,0:T(8,128)(2,1)S(1)}, bf16[1,8,384,384]{3,2,1,0:T(8,128)(2,1)}, u32[]{:S(2)}) copy-start(bf16[1,8,384,384]{3,2,1,0:T(8,128)(2,1)} %param.20) | copy-start | bytes 7077892
  7.2 5.2 %copy-start.2 = (f32[1,16,4352]{2,1,0:T(8,128)S(1)}, f32[1,16,4352]{2,1,0:T(8,128)}, u32[]{:S(2)}) copy-start(f32[1,16,4352]{2,1,0:T(8,128)} %param.13) | copy-start | bytes 835588
  7.2 5.2 %copy-start.4 = (s32[1,128]{1,0:T(1,128)S(1)}, s32[1,128]{1,0:T(1,128)}, u32[]{:S(2)}) copy-start(s32[1,128]{1,0:T(1,128)} %param.17) | copy-start | bytes 1540
  7.2 5.3 %copy-start.5 = (s32[1,8]{1,0:T(1,128)S(1)}, s32[1,8]{1,0:T(1,128)}, u32[]{:S(2)}) copy-start(s32[1,8]{1,0:T(1,128)} %param.18) | copy-start | bytes 100
  7.2 144.1 %all-reduce.3.cloned.1.call-start = ((), (), s32[]{:S(2)}) async-start(), calls=%async_computation.1 | async-start | bytes 131072 | tf_op jit(solution)/shard_map/psum | solution.py:59
  15.3 257.9 %copy-start.1 = (bf16[1,4352,128]{2,1,0:T(8,128)(2,1)S(1)}, bf16[1,4352,128]{2,1,0:T(8,128)(2,1)}, u32[]{:S(2)}) copy-start(bf16[1,4352,128]{2,1,0:T(8,128)(2,1)} %param.22) | copy-start | bytes 3342340
  231.1 3.3 %copy-start.3 = (f32[64,512]{1,0:T(8,128)S(1)}, f32[64,512]{1,0:T(8,128)}, u32[]{:S(2)}) copy-start(f32[64,512]{1,0:T(8,128)} %param.23) | copy-start | bytes 393220
  276.5 22.0 %collective-permute-start = (f32[16,1,128]{2,1,0:T(1,128)S(1)}, f32[16,1,128]{2,1,0:T(1,128)S(1)}, u32[]{:S(2)}, u32[]{:S(2)}) collective-permute-start(f32[16,1,128]{2,1,0:T(1,128)S(1)} %get-tuple-element.4), channel_id=1, source_target_pairs={{0,32},{32,64},{64,96},{96,128},{128,160},{160,192},{192,224},{1,3... | collective-permute-start | bytes 24584 | tf_op jit(solution)/shard_map/ppermute | solution.py:15
  289.2 9.3 %collective-permute-start.1 = (f32[16,1,128]{2,1,0:T(1,128)S(1)}, f32[16,1,128]{2,1,0:T(1,128)S(1)}, u32[]{:S(2)}, u32[]{:S(2)}) collective-permute-start(f32[16,1,128]{2,1,0:T(1,128)S(1)} %get-tuple-element.5), channel_id=1, source_target_pairs={{32,0},{64,32},{96,64},{128,96},{160,128},{192,160},{224,192},{33,... | collective-permute-start | bytes 24584 | tf_op jit(solution)/shard_map/ppermute | solution.py:17
  291.9 15.5 %all-to-all-start = ((bf16[16,32,128]{2,0,1:T(8,128)(2,1)}), bf16[16,32,128]{2,0,1:T(8,128)(2,1)S(1)}, u32[]{:S(2)}, u32[]{:S(2)}) async-start(bf16[16,32,128]{2,0,1:T(8,128)(2,1)} %copy.36), calls=%async_computation | async-start | bytes 262144 | tf_op jit(solution)/shard_map/all_to_all | solution.py:79
Sparse Core Ops, SparseCore 0:
  12.5 138.7 all-reduce.2
where the time goes:
time: 319 us
  waiting for transfers between devices  145 us (45%)
  blocking collectives  113 us (35%)
  starting transfers between devices  20.3 us (6%)
  matrix products  15 us (5%)
  between operations  14.3 us (4%)
  local copies, waits for them, and re-layouts  9.48 us (3%)
    psum x1, waiting for transfers between devices, shards(): level2 = lax.psum(contrib.astype(jnp.bfloat16), 'sub').astype(jnp.float32)  136 us
    psum x1, blocking collectives, shards(): level3 = lax.psum(top_term, ('group', 'sub'))  78 us
    all_gather x1, blocking collectives, shards(): lax.all_gather(coarse2_mine.astype(jnp.bfloat16), 'sub', axis=1, tiled=True)  35 us
    ppermute x1, starting transfers between devices, padded_2(): lax.ppermute(tail, axis, [(i, (i + 1) % count) for i in range(ends)])  12.7 us
    all_to_all x1, waiting for transfers between devices, shards(): lax.all_to_all(slots[:, :nsub, :].astype(jnp.bfloat16), 'sub', split_axis...  8.85 us
  transfers between devices with their start and end apart: 4, of which 2 were waited for; matrix products, arithmetic and copies ran while one was open for 1% of the time, Pallas kernels for 0%

commit v1 on v0

--- a/solution.py
+++ b/solution.py
@@ -2,6 +2,18 @@
 import jax.numpy as jnp
 from jax import lax
 from jax.sharding import PartitionSpec as P
+
+
+def collect(value, axis, dim):
+    ways, here = (lax.axis_size(axis), lax.axis_index(axis))
+    grown, reach = (value, 1)
+    while reach < ways:
+        theirs = lax.ppermute(grown, axis, [(d, d ^ reach) for d in range(ways)])
+        mine_first = jnp.concatenate([grown, theirs], axis=dim)
+        theirs_first = jnp.concatenate([theirs, grown], axis=dim)
+        grown = jnp.where(here & reach == 0, mine_first, theirs_first)
+        reach = 2 * reach
+    return grown
 
 
 def padded_2(cells, sides, width):
@@ -69,7 +81,7 @@
     coarse3 = jnp.dot(level3, top_inverse, precision=highest)
     lifted = lax.dot_general(coarse3, group_basis, (((1,), (1,)), ((), ())), precision=highest)
     coarse2_mine = jnp.dot(level2, group_inverse, precision=highest) + lifted
-    coarse2 = lax.all_gather(coarse2_mine.astype(jnp.bfloat16), "sub", axis=1, tiled=True)
+    coarse2 = collect(coarse2_mine.astype(jnp.bfloat16), "sub", 1)
     values = jnp.take(coarse2, own2[0], axis=1)
     spread = lax.dot_general(
         values, coarse_basis[0], (((1,), (1,)), ((), ())), preferred_element_type=jnp.float32

time: 319 us -> 298 us (0.934)
  blocking collectives: 113 us -> 78 us
  starting transfers between devices: 20.3 us -> 24.8 us
  other arithmetic: 1.78 us -> 6 us
    all_gather x1 -> x0, blocking collectives: 35 us -> none  [shards(): lax.all_gather(coarse2_mine.astype(jnp.bfloat16), 'sub', axis=1, tiled=True)]
    all_to_all x1, waiting for transfers between devices: 8.85 us -> 0.01 us  [shards(): lax.all_to_all(slots[:, :nsub, :].astype(jnp.bfloat16), 'sub', split_axis...]
    ppermute x0 -> x5, waiting for transfers between devices: none -> 8.61 us  [collect(): theirs = lax.ppermute(grown, axis, [(d, d ^ reach) for d in range(ways)])]
    ppermute x0 -> x5, starting transfers between devices: none -> 7.55 us  [collect(): theirs = lax.ppermute(grown, axis, [(d, d ^ reach) for d in range(ways)])]
    ppermute x1, starting transfers between devices: 12.7 us -> 8.56 us  [padded_2(): lax.ppermute(tail, axis, [(i, (i + 1) % count) for i in range(ends)])]
  transfers between devices with their start and end apart: 4 -> 9, of which waited for: 2 -> 7; matrix products, arithmetic and copies ran while one was open for 1% -> 2% of each run, Pallas kernels for 0% -> 0%
where the time goes in v1:
time: 298 us; the launch traced here: 296 us
  waiting for transfers between devices  147 us (49%)
  blocking collectives  78 us (26%)
  starting transfers between devices  24.8 us (8%)
  matrix products  15.8 us (5%)
  between operations  14.2 us (5%)
  local copies, waits for them, and re-layouts  10.3 us (3%)
  other arithmetic  6 us (2%)
    psum x1, waiting for transfers between devices, shards(): level2 = lax.psum(contrib.astype(jnp.bfloat16), 'sub').astype(jnp.float32)  136 us
    psum x1, blocking collectives, shards(): level3 = lax.psum(top_term, ('group', 'sub'))  78 us
    ppermute x5, waiting for transfers between devices, collect(): theirs = lax.ppermute(grown, axis, [(d, d ^ reach) for d in range(ways)])  8.61 us
    ppermute x1, starting transfers between devices, padded_2(): lax.ppermute(tail, axis, [(i, (i + 1) % count) for i in range(ends)])  8.56 us
    ppermute x5, starting transfers between devices, collect(): theirs = lax.ppermute(grown, axis, [(d, d ^ reach) for d in range(ways)])  7.55 us
    all_to_all x1, starting transfers between devices, shards(): lax.all_to_all(slots[:, :nsub, :].astype(jnp.bfloat16), 'sub', split_axis...  6.7 us
  transfers between devices with their start and end apart: 9, of which 7 were waited for; matrix products, arithmetic and copies ran while one was open for 2% of the time, Pallas kernels for 0%

profile of v1, /device:TPU:1, one launch (start us, length us, event | category | flops | bytes accessed | tf_op | source)
XLA Modules:
  0.0 296.2 jit_solution(9560376751784111138)
XLA Ops:
  7.2 0.0 copy-start
  7.2 0.0 copy-start.2
  7.2 0.0 all-reduce.3.cloned.1.call-start
  7.2 0.8 convert_bitcast_fusion
  8.1 0.1 broadcast_bitcast_fusion
  8.2 0.8 fusion.44
  8.9 1.6 fusion.25
  10.5 1.8 convolution_convert_fusion
  12.3 0.0 all-reduce.3.cloned.1.call-update
  12.4 0.0 copy-done.2
  12.4 0.0 copy-start.3
  12.5 2.8 fusion.7
  15.3 0.0 copy-start.4
  15.3 0.0 copy-start.5
  15.3 136.0 %all-reduce.3.cloned.1.call-done = bf16[16,2048]{1,0:T(8,128)(2,1)} async-done(((bf16[16,2048]{1,0:T(8,128)(2,1)}), bf16[16,2048]{1,0:T(8,128)(2,1)}) %all-reduce.3.cloned.1.call-update) | async-done | bytes 65552 | tf_op jit(solution)/shard_map/psum | solution.py:71
  151.3 0.0 copy-done.3
  151.3 0.9 fusion.46
  152.2 78.0 %psum.15 = f32[16,512]{1,0:T(8,128)S(1)} all-reduce(f32[16,512]{1,0:T(8,128)S(1)} %fusion.46), channel_id=1, replica_groups=mesh['group'=8,'sub'=32] {'group','sub'}, use_global_device_ids=true, to_apply=%region_1.0 | all-reduce | flops 8192 | bytes 65536 | tf_op jit(solution)/shard_map/psum | solution.py:80
  230.2 0.0 copy-start.1
  230.2 1.9 fusion.57
  232.1 1.4 fusion.56
  233.5 1.1 fusion.27
  234.7 1.6 collective-permute-start
  236.2 0.0 copy-done.4
  236.2 0.5 fusion.48
  236.7 0.5 collective-permute-done
  237.2 0.1 maximum_select_fusion.4
  237.3 0.1 collective-permute-start.1
  237.4 3.2 %collective-permute-done.1 = bf16[16,128]{1,0:T(8,128)(2,1)S(1)} collective-permute-done((bf16[16,128]{1,0:T(8,128)(2,1)S(1)}, bf16[16,128]{1,0:T(8,128)(2,1)S(1)}, u32[]{:S(2)}, u32[]{:S(2)}) %collective-permute-start.1) | collective-permute-done | bytes 4128 | tf_op jit(solution)/shard_map/ppermute | solution.py:11
  240.7 3.2 %collective-permute-start.2 = (bf16[16,256]{1,0:T(8,128)(2,1)S(1)}, bf16[16,256]{1,0:T(8,128)(2,1)S(1)}, u32[]{:S(2)}, u32[]{:S(2)}) collective-permute-start(bf16[16,256]{1,0:T(8,128)(2,1)S(1)} %maximum_select_fusion.3), channel_id=1, source_target_pairs={{0,4},{1,5},{2,6},{3,7},{4,0},{5,1},{6,2},{7,3},{8,12},{9,13},{10,... | collective-permute-start | bytes 24584 | tf_op jit(solution)/shard_map/ppermute | solution.py:11
  243.9 0.0 copy-done.5
  243.9 3.2 %collective-permute-done.2 = bf16[16,256]{1,0:T(8,128)(2,1)S(1)} collective-permute-done((bf16[16,256]{1,0:T(8,128)(2,1)S(1)}, bf16[16,256]{1,0:T(8,128)(2,1)S(1)}, u32[]{:S(2)}, u32[]{:S(2)}) %collective-permute-start.2) | collective-permute-done | bytes 8224 | tf_op jit(solution)/shard_map/ppermute | solution.py:11
  247.1 0.8 collective-permute-start.3
  247.9 0.7 compare_and_fusion
  248.6 1.4 collective-permute-done.3
  250.0 0.8 maximum_select_fusion.1
  250.8 1.9 collective-permute-start.4
  252.6 0.7 pad_clamp_fusion.1
  253.3 1.7 copy.39
  255.0 0.3 collective-permute-done.4
  255.2 1.5 maximum_select_fusion
  256.7 1.8 copy.33
  258.6 1.8 gather_fusion
  260.3 0.0 copy-done.1
  260.3 2.2 fusion
  262.5 1.0 reshape.101
  263.6 0.7 copy.34
  264.3 6.7 %all-to-all-start = ((bf16[16,32,128]{2,0,1:T(8,128)(2,1)}), bf16[16,32,128]{2,0,1:T(8,128)(2,1)S(1)}, u32[]{:S(2)}, u32[]{:S(2)}) async-start(bf16[16,32,128]{2,0,1:T(8,128)(2,1)} %copy.34), calls=%async_computation | async-start | bytes 262144 | tf_op jit(solution)/shard_map/all_to_all | solution.py:91
  271.0 8.6 %collective-permute-start.5 = (f32[16,1,128]{2,1,0:T(1,128)S(1)}, f32[16,1,128]{2,1,0:T(1,128)S(1)}, u32[]{:S(2)}, u32[]{:S(2)}) collective-permute-start(f32[16,1,128]{2,1,0:T(1,128)S(1)} %get-tuple-element.4), channel_id=1, source_target_pairs={{0,32},{32,64},{64,96},{96,128},{128,160},{160,192},{192,224},{1,3... | collective-permute-start | bytes 24584 | tf_op jit(solution)/shard_map/ppermute | solution.py:27
  279.6 1.9 collective-permute-start.6
  281.5 1.0 copy.41
  282.5 0.0 collective-permute-done.5
  282.5 2.3 collective-permute-done.6
  284.9 0.0 all-to-all-done
  285.0 0.1 convert_element_type.48
  285.1 0.6 gather_fusion.1
  285.6 0.0 copy-done
  285.7 2.1 fusion.10
  287.8 0.1 copy.38
  287.9 0.7 broadcast_in_dim_reshape.7
  288.6 0.8 broadcast_in_dim_reshape.6
  (16 shorter events, 0.3 us)
Async XLA Ops:
  7.2 278.5 %copy-start = (bf16[1,8,384,384]{3,2,1,0:T(8,128)(2,1)S(1)}, bf16[1,8,384,384]{3,2,1,0:T(8,128)(2,1)}, u32[]{:S(2)}) copy-start(bf16[1,8,384,384]{3,2,1,0:T(8,128)(2,1)} %param.20) | copy-start | bytes 7077892
  7.2 5.2 %copy-start.2 = (f32[1,16,4352]{2,1,0:T(8,128)S(1)}, f32[1,16,4352]{2,1,0:T(8,128)}, u32[]{:S(2)}) copy-start(f32[1,16,4352]{2,1,0:T(8,128)} %param.13) | copy-start | bytes 835588
  7.2 144.1 %all-reduce.3.cloned.1.call-start = ((), (), s32[]{:S(2)}) async-start(), calls=%async_computation.1 | async-start | bytes 131072 | tf_op jit(solution)/shard_map/psum | solution.py:71
  12.4 138.9 %copy-start.3 = (f32[64,512]{1,0:T(8,128)S(1)}, f32[64,512]{1,0:T(8,128)}, u32[]{:S(2)}) copy-start(f32[64,512]{1,0:T(8,128)} %param.23) | copy-start | bytes 393220
  15.3 220.9 %copy-start.4 = (s32[1,128]{1,0:T(1,128)S(1)}, s32[1,128]{1,0:T(1,128)}, u32[]{:S(2)}) copy-start(s32[1,128]{1,0:T(1,128)} %param.17) | copy-start | bytes 1540
  15.3 228.6 %copy-start.5 = (s32[1,8]{1,0:T(1,128)S(1)}, s32[1,8]{1,0:T(1,128)}, u32[]{:S(2)}) copy-start(s32[1,8]{1,0:T(1,128)} %param.18) | copy-start | bytes 100
  230.2 30.2 %copy-start.1 = (bf16[1,4352,128]{2,1,0:T(8,128)(2,1)S(1)}, bf16[1,4352,128]{2,1,0:T(8,128)(2,1)}, u32[]{:S(2)}) copy-start(bf16[1,4352,128]{2,1,0:T(8,128)(2,1)} %param.22) | copy-start | bytes 3342340
  234.7 2.6 collective-permute-start
  237.3 3.4 %collective-permute-start.1 = (bf16[16,128]{1,0:T(8,128)(2,1)S(1)}, bf16[16,128]{1,0:T(8,128)(2,1)S(1)}, u32[]{:S(2)}, u32[]{:S(2)}) collective-permute-start(bf16[16,128]{1,0:T(8,128)(2,1)S(1)} %maximum_select_fusion.4), channel_id=1, source_target_pairs={{0,2},{1,3},{2,0},{3,1},{4,6},{5,7},{6,4},{7,5},{8,10},{9,11},{10,... | collective-permute-start | bytes 12296 | tf_op jit(solution)/shard_map/ppermute | solution.py:11
  240.7 6.4 %collective-permute-start.2 = (bf16[16,256]{1,0:T(8,128)(2,1)S(1)}, bf16[16,256]{1,0:T(8,128)(2,1)S(1)}, u32[]{:S(2)}, u32[]{:S(2)}) collective-permute-start(bf16[16,256]{1,0:T(8,128)(2,1)S(1)} %maximum_select_fusion.3), channel_id=1, source_target_pairs={{0,4},{1,5},{2,6},{3,7},{4,0},{5,1},{6,2},{7,3},{8,12},{9,13},{10,... | collective-permute-start | bytes 24584 | tf_op jit(solution)/shard_map/ppermute | solution.py:11
  247.1 2.9 collective-permute-start.3
  250.8 4.5 %collective-permute-start.4 = (bf16[16,1024]{1,0:T(8,128)(2,1)S(1)}, bf16[16,1024]{1,0:T(8,128)(2,1)}, u32[]{:S(2)}, u32[]{:S(2)}) collective-permute-start(bf16[16,1024]{1,0:T(8,128)(2,1)S(1)} %maximum_select_fusion.1), channel_id=1, source_target_pairs={{0,16},{1,17},{2,18},{3,19},{4,20},{5,21},{6,22},{7,23},{8,24},{9,... | collective-permute-start | bytes 98312 | tf_op jit(solution)/shard_map/ppermute | solution.py:11
  264.3 20.6 %all-to-all-start = ((bf16[16,32,128]{2,0,1:T(8,128)(2,1)}), bf16[16,32,128]{2,0,1:T(8,128)(2,1)S(1)}, u32[]{:S(2)}, u32[]{:S(2)}) async-start(bf16[16,32,128]{2,0,1:T(8,128)(2,1)} %copy.34), calls=%async_computation | async-start | bytes 262144 | tf_op jit(solution)/shard_map/all_to_all | solution.py:91
  271.0 11.5 %collective-permute-start.5 = (f32[16,1,128]{2,1,0:T(1,128)S(1)}, f32[16,1,128]{2,1,0:T(1,128)S(1)}, u32[]{:S(2)}, u32[]{:S(2)}) collective-permute-start(f32[16,1,128]{2,1,0:T(1,128)S(1)} %get-tuple-element.4), channel_id=1, source_target_pairs={{0,32},{32,64},{64,96},{96,128},{128,160},{160,192},{192,224},{1,3... | collective-permute-start | bytes 24584 | tf_op jit(solution)/shard_map/ppermute | solution.py:27
  279.6 5.3 %collective-permute-start.6 = (f32[16,1,128]{2,1,0:T(1,128)S(1)}, f32[16,1,128]{2,1,0:T(1,128)S(1)}, u32[]{:S(2)}, u32[]{:S(2)}) collective-permute-start(f32[16,1,128]{2,1,0:T(1,128)S(1)} %get-tuple-element.5), channel_id=1, source_target_pairs={{32,0},{64,32},{96,64},{128,96},{160,128},{192,160},{224,192},{33,... | collective-permute-start | bytes 24584 | tf_op jit(solution)/shard_map/ppermute | solution.py:29
Sparse Core Ops, SparseCore 0:
  12.5 138.7 all-reduce.2
